TPU v7x, 32 devices: a whole 2x2x4 slice. The times are simulated.
32 devices in a mesh: recv: 8 (over z, y), tm: 4 (over x, core).
Axes of the slice: x: 2, y: 2, z: 4, core: 2. Of those that a mesh axis runs over, the one named last changes fastest.
Arguments:
- spectra: bfloat16 [2, 128, 64, 512], P(None, 'tm', 'recv'), may hold values from -6 to 6
- owners: int32 [4], replicated, may hold values from 0 to 7
- source_slots: int32 [4, 8], replicated, may hold values from 0 to 7, as said below
Outputs:
- correlations: float32 [32, 64, 512], P('tm', 'recv')
Inputs may be any that keep to these rules, and one draw needn't show every extreme that they name: Block k of sources lies among the channels of recv index owners[k]. `source_slots`: the 8 slots of one block are distinct.
All inputs are finite; a program needn't handle non-finite values.
Results may differ from a plain program's by a relative error of at most 0.0019.
Values may be sent and summed in bfloat16 or wider, within the bound.
A program may use at most 64 MiB of HBM per device.

v0:
```python
import math

import jax
import jax.numpy as jnp
from jax import lax
from jax.sharding import PartitionSpec as P

HALF = 64
STEPS = 4


epsilon = 1e-05


def broadcast(value, axis, source):
    kept = jnp.where(lax.axis_index(axis) == source, value, 0).astype(value.dtype)
    return lax.psum(kept, axis)


def band_matrix(length, half_width):
    positions = lax.iota(jnp.int32, length)
    near = (jnp.abs(positions[:, None] - positions[None, :]) <= half_width).astype(jnp.float32)
    return near / jnp.sum(near, axis=0, keepdims=True)


def transform_tables(length):
    positions = lax.iota(jnp.int32, length)
    phase = positions[:, None] * positions[None, :] % length
    angle = phase.astype(jnp.float32) * (2.0 * math.pi / length)
    return (jnp.cos(angle), jnp.sin(angle))


def inverse_lags(cross_real, cross_imag, cosine, sine):
    length = cross_real.shape[-1]
    high = lax.Precision.HIGHEST
    flat_real = cross_real.reshape(-1, length)
    flat_imag = cross_imag.reshape(-1, length)
    lag_terms = jnp.dot(
        flat_real, cosine, precision=high, preferred_element_type=jnp.float32
    ) - jnp.dot(flat_imag, sine, precision=high, preferred_element_type=jnp.float32)
    return (lag_terms / length).reshape(cross_real.shape)


def per_device(spectra, owners, source_slots):
    length = spectra.shape[3]
    width = spectra.shape[2]
    band_table = band_matrix(length, HALF)
    parts = spectra.astype(jnp.float32)
    energy = parts[0] * parts[0] + parts[1] * parts[1]
    smooth = jnp.dot(
        energy.reshape(-1, length),
        band_table,
        precision=lax.Precision.HIGHEST,
        preferred_element_type=jnp.float32,
    ).reshape(energy.shape)
    whitened = (parts * lax.rsqrt(smooth + epsilon)[None]).astype(jnp.bfloat16)
    positions = lax.iota(jnp.int32, width)
    real_parts = []
    imag_parts = []
    for step in range(STEPS):
        selector = (source_slots[step][:, None] == positions[None, :]).astype(jnp.bfloat16)
        picked = jnp.einsum(
            "sr,cwrf->cwsf", selector, whitened, preferred_element_type=jnp.float32
        ).astype(jnp.bfloat16)
        arrived = broadcast(picked, "recv", owners[step])
        real_parts.append(
            jnp.einsum("wsf,wrf->srf", arrived[0], whitened[0], preferred_element_type=jnp.float32)
            + jnp.einsum(
                "wsf,wrf->srf", arrived[1], whitened[1], preferred_element_type=jnp.float32
            )
        )
        imag_parts.append(
            jnp.einsum("wsf,wrf->srf", arrived[0], whitened[1], preferred_element_type=jnp.float32)
            - jnp.einsum(
                "wsf,wrf->srf", arrived[1], whitened[0], preferred_element_type=jnp.float32
            )
        )
    cross_real = jnp.concatenate(real_parts, axis=0)
    cross_imag = jnp.concatenate(imag_parts, axis=0)
    cosine, sine = transform_tables(length)
    return lax.psum_scatter(
        inverse_lags(cross_real, cross_imag, cosine, sine), "tm", scatter_dimension=0, tiled=True
    )


def solution(mesh):
    in_specs = (P(None, "tm", "recv", None), P(), P())
    out_specs = P("tm", "recv", None)
    return jax.shard_map(
        per_device, mesh=mesh, in_specs=in_specs, out_specs=out_specs, check_vma=False
    )
```

profile of v0, /device:TPU:0, one launch (start us, length us, event | category | flops | bytes accessed | tf_op | source)
XLA Modules:
  0.0 247.8 jit_solution(7423149175860484933)
XLA Ops:
  19.7 104.5 %all-reduce.3.cloned.1.call-done = (bf16[2,32,8,512]{3,2,1,0:T(8,128)(2,1)}, bf16[2,32,8,512]{3,2,1,0:T(8,128)(2,1)}, bf16[2,32,8,512]{3,2,1,0:T(8,128)(2,1)}, bf16[2,32,8,512]{3,2,1,0:T(8,128)(2,1)}) async-done(((bf16[2,32,8,512]{3,2,1,0:T(8,128)(2,1)}, bf16[2,32,8,512]{3,2,1,0:T(8,128)(2,1)}, bf16[2,32,8,512]{3,2,1,0:T(8,128)(2,1)}, bf16[2,32,8,512]{3,2,1,0:T(8,128)(2,1)}), ...) | async-done | bytes 2097168 | tf_op jit(solution)/shard_map/psum | solution.py:17
  124.2 2.1 slice_bitcast_fusion.4
  129.9 2.0 fusion.69
  131.9 2.1 fusion.70
  134.0 2.0 fusion.65
  136.0 2.1 fusion.66
  139.1 1.8 copy.92
  140.9 2.1 fusion.67
  143.0 2.0 fusion.71
  145.0 1.8 copy.96
  146.8 2.0 fusion.68
  148.9 2.0 fusion.72
  152.7 3.6 %subtract_bitcast_fusion.3 = f32[8,8,512]{0,1,2:T(8,128)} fusion(f32[512,8,8]{2,1,0:T(8,128)} %fusion.69, bf16[32,8,512]{0,1,2:T(8,128)(2,1)S(1)} %copy.83, bf16[32,8,512]{0,1,2:T(8,128)(2,1)S(1)} %copy.86), kind=kOutput, calls=%fused_computation.3 | convolution fusion | flops 2129920 | bytes 786432 | tf_op jit(solution)/shard_map/wsf,wrf->srf/dot_general | solution.py:74
  156.3 2.2 copy.119
  158.5 3.0 %copy.90 = bf16[32,8,512]{0,1,2:T(8,128)(2,1)} copy(bf16[32,8,512]{2,1,0:T(8,128)(2,1)} %get-tuple-element.11) | data formatting | bytes 524288 | tf_op jit(solution)/shard_map/squeeze | solution.py:69
  161.4 3.9 %subtract_bitcast_fusion.2 = f32[8,8,512]{0,1,2:T(8,128)} fusion(f32[512,8,8]{2,1,0:T(8,128)} %fusion.70, bf16[32,8,512]{0,1,2:T(8,128)(2,1)S(1)} %copy.83, bf16[32,8,512]{0,1,2:T(8,128)(2,1)} %copy.90), kind=kOutput, calls=%fused_computation.2 | convolution fusion | flops 2129920 | bytes 786432 | tf_op jit(solution)/shard_map/wsf,wrf->srf/dot_general | solution.py:74
  165.4 2.8 %copy.120 = f32[8,8,512]{2,1,0:T(8,128)} copy(f32[8,8,512]{0,1,2:T(8,128)} %subtract_bitcast_fusion.2) | data formatting | bytes 262144 | tf_op jit(solution)/shard_map/sub | solution.py:73
  168.2 3.6 %add_bitcast_fusion.3 = f32[8,8,512]{0,1,2:T(8,128)} fusion(f32[512,8,8]{2,1,0:T(8,128)} %fusion.65, bf16[32,8,512]{0,1,2:T(8,128)(2,1)S(1)} %copy.85, bf16[32,8,512]{0,1,2:T(8,128)(2,1)S(1)} %copy.86), kind=kOutput, calls=%fused_computation.7 | convolution fusion | flops 2129920 | bytes 786432 | tf_op jit(solution)/shard_map/wsf,wrf->srf/dot_general | solution.py:68
  171.8 2.9 %copy.99 = f32[8,8,512]{2,1,0:T(8,128)} copy(f32[8,8,512]{0,1,2:T(8,128)} %add_bitcast_fusion.3) | data formatting | bytes 262144 | tf_op jit(solution)/shard_map/add | solution.py:67
  174.8 3.6 %add_bitcast_fusion.2 = f32[8,8,512]{0,1,2:T(8,128)} fusion(f32[512,8,8]{2,1,0:T(8,128)} %fusion.66, bf16[32,8,512]{0,1,2:T(8,128)(2,1)S(1)} %copy.85, bf16[32,8,512]{0,1,2:T(8,128)(2,1)S(1)} %copy-done.1), kind=kOutput, calls=%fused_computation.6 | convolution fusion | flops 2129920 | bytes 786432 | tf_op jit(solution)/shard_map/wsf,wrf->srf/dot_general | solution.py:68
  178.4 2.8 %copy.100 = f32[8,8,512]{2,1,0:T(8,128)} copy(f32[8,8,512]{0,1,2:T(8,128)} %add_bitcast_fusion.2) | data formatting | bytes 262144 | tf_op jit(solution)/shard_map/add | solution.py:67
  183.0 3.7 %add_bitcast_fusion.1 = f32[8,8,512]{0,1,2:T(8,128)} fusion(f32[512,8,8]{2,1,0:T(8,128)} %fusion.67, bf16[32,8,512]{0,1,2:T(8,128)(2,1)S(1)} %copy.85, bf16[32,8,512]{0,1,2:T(8,128)(2,1)S(1)} %copy.94), kind=kOutput, calls=%fused_computation.5 | convolution fusion | flops 2129920 | bytes 786432 | tf_op jit(solution)/shard_map/wsf,wrf->srf/dot_general | solution.py:68
  186.7 2.8 %copy.101 = f32[8,8,512]{2,1,0:T(8,128)} copy(f32[8,8,512]{0,1,2:T(8,128)} %add_bitcast_fusion.1) | data formatting | bytes 262144 | tf_op jit(solution)/shard_map/add | solution.py:67
  191.3 3.9 %add_bitcast_fusion = f32[8,8,512]{0,1,2:T(8,128)} fusion(f32[512,8,8]{2,1,0:T(8,128)} %fusion.68, bf16[32,8,512]{0,1,2:T(8,128)(2,1)S(1)} %copy.85, bf16[32,8,512]{0,1,2:T(8,128)(2,1)} %copy.98), kind=kOutput, calls=%fused_computation.4 | convolution fusion | flops 2129920 | bytes 786432 | tf_op jit(solution)/shard_map/wsf,wrf->srf/dot_general | solution.py:68
  195.2 2.2 copy.102
  197.4 3.6 %subtract_bitcast_fusion.1 = f32[8,8,512]{0,1,2:T(8,128)} fusion(f32[512,8,8]{2,1,0:T(8,128)} %fusion.71, bf16[32,8,512]{0,1,2:T(8,128)(2,1)S(1)} %copy.83, bf16[32,8,512]{0,1,2:T(8,128)(2,1)S(1)} %copy.94), kind=kOutput, calls=%fused_computation.1 | convolution fusion | flops 2129920 | bytes 786432 | tf_op jit(solution)/shard_map/wsf,wrf->srf/dot_general | solution.py:74
  201.0 2.3 copy.121
  203.3 3.6 %subtract_bitcast_fusion = f32[8,8,512]{0,1,2:T(8,128)} fusion(f32[512,8,8]{2,1,0:T(8,128)} %fusion.72, bf16[32,8,512]{0,1,2:T(8,128)(2,1)S(1)} %copy.83, bf16[32,8,512]{0,1,2:T(8,128)(2,1)S(1)} %copy-done), kind=kOutput, calls=%fused_computation | convolution fusion | flops 2129920 | bytes 786432 | tf_op jit(solution)/shard_map/wsf,wrf->srf/dot_general | solution.py:74
  206.9 2.2 copy.122
  209.2 5.1 %fusion.17 = f32[256,512]{1,0:T(8,128)S(1)} fusion(f32[8,8,512]{2,1,0:T(8,128)S(1)} %copy.102, f32[8,8,512]{2,1,0:T(8,128)S(1)} %copy-done.9, f32[8,8,512]{2,1,0:T(8,128)S(1)} %copy-done.8, f32[8,8,512]{2,1,0:T(8,128)S(1)} %copy-done.7), kind=kOutput, calls=%fused_computation.35 | convolution fusion | flops 809369600 | bytes 1048576 | tf_op jit(solution)/shard_map/dot_general | solution.py:38
  214.3 5.7 %fusion.2 = f32[32,8,512]{2,1,0:T(8,128)} fusion(f32[256,512]{1,0:T(8,128)S(1)} %fusion.17, f32[8,8,512]{2,1,0:T(8,128)S(1)} %copy.122, f32[8,8,512]{2,1,0:T(8,128)S(1)} %copy.121, f32[8,8,512]{2,1,0:T(8,128)S(1)} %copy-done.6, f32[8,8,512]{2,1,0:T(8,128)S(1)} %copy.119), kind=kOutput, calls=%fused_computation.21 | convolution fusion | flops 809631744 | bytes 1572864 | tf_op jit(solution)/shard_map/dot_general | solution.py:40
  220.1 20.9 %reduce-scatter.2.cloned.1.call-done = f32[8,8,512]{2,1,0:T(8,128)} async-done(((f32[32,8,512]{2,1,0:T(8,128)}), f32[8,8,512]{2,1,0:T(8,128)}) %reduce-scatter.2.cloned.1.call-update) | async-done | bytes 131088 | tf_op jit(solution)/shard_map/reduce_scatter | solution.py:81
  (45 shorter events, 20.5 us)
Async XLA Ops:
  6.5 117.7 %all-reduce.3.cloned.1.call-start = ((), (), s32[]{:S(2)}) async-start(), calls=%async_computation.2 | async-start | bytes 4194304 | tf_op jit(solution)/shard_map/psum | solution.py:17
  9.3 1.2 copy-start.3
  9.3 1.3 copy-start.10
  17.7 223.3 %reduce-scatter.2.cloned.1.call-start = ((), (), s32[]{:S(2)}) async-start(), calls=%async_computation.1 | async-start | bytes 655360 | tf_op jit(solution)/shard_map/reduce_scatter | solution.py:81
  129.9 2.0 copy-start.2
  136.0 2.2 copy-start.4
  136.0 2.2 copy-start.5
  171.8 2.9 %copy-start.1 = (bf16[32,8,512]{0,1,2:T(8,128)(2,1)S(1)}, bf16[32,8,512]{0,1,2:T(8,128)(2,1)}, u32[]{:S(2)}) copy-start(bf16[32,8,512]{0,1,2:T(8,128)(2,1)} %copy.90) | copy-start | bytes 786436
  201.0 2.3 copy-start
  206.9 2.2 copy-start.7
  206.9 2.3 copy-start.8
  206.9 2.3 copy-start.9
  209.2 5.2 %copy-start.6 = (f32[8,8,512]{2,1,0:T(8,128)S(1)}, f32[8,8,512]{2,1,0:T(8,128)}, u32[]{:S(2)}) copy-start(f32[8,8,512]{2,1,0:T(8,128)} %copy.120) | copy-start | bytes 393220
Sparse Core Ops, SparseCore 0:
  17.8 106.3 all-reduce.2
  220.2 20.7 reduce-scatter.1
where the time goes:
time: 249 us; the launch traced here: 248 us
  waiting for transfers between devices  125 us (50%)
  matrix products  62.6 us (25%)
  local copies, waits for them, and re-layouts  42.1 us (17%)
  between operations  16.1 us (6%)
    psum x1, waiting for transfers between devices, broadcast(): return lax.psum(kept, axis)  105 us
    reduce_scatter x1, waiting for transfers between devices, per_device(): lax.psum_scatter(inverse_lags(cross_real, cross_imag, cosine, sine), 'tm'...  20.9 us
    dot_general x4, matrix products, per_device(): jnp.einsum('wsf,wrf->srf', arrived[1], whitened[1], preferred_element_typ...  14.8 us
    dot_general x4, matrix products, per_device(): jnp.einsum('wsf,wrf->srf', arrived[1], whitened[0], preferred_element_typ...  14.7 us
    squeeze x6, local copies, waits for them, and re-layouts, per_device(): arrived[1]  11.4 us
    add x4, local copies, waits for them, and re-layouts, per_device(): jnp.einsum('wsf,wrf->srf', arrived[0], whitened[0], preferred_element_typ...  10.8 us
    sub x4, local copies, waits for them, and re-layouts, per_device(): jnp.einsum('wsf,wrf->srf', arrived[0], whitened[1], preferred_element_typ...  9.53 us
    dot_general x4, matrix products, per_device(): jnp.einsum('wsf,wrf->srf', arrived[0], whitened[0], preferred_element_typ...  8.25 us
  transfers between devices with their start and end apart: 2, of which 2 were waited for; matrix products, arithmetic and copies ran while one was open for 1% of the time, Pallas kernels for 0%

commit v1 on v0

--- a/solution.py
+++ b/solution.py
@@ -2,14 +2,20 @@
 
 import jax
 import jax.numpy as jnp
+import numpy as np
 from jax import lax
+from jax.experimental import pallas as pl
+from jax.experimental.pallas import tpu as pltpu
 from jax.sharding import PartitionSpec as P
 
 HALF = 64
 STEPS = 4
-
+BINS = 16
+PAIRS = BINS // 2
 
 epsilon = 1e-05
+MESH = pl.DeviceIdType.MESH
+NT = (((1,), (1,)), ((), ()))
 
 
 def broadcast(value, axis, source):
@@ -41,7 +47,7 @@
     return (lag_terms / length).reshape(cross_real.shape)
 
 
-def per_device(spectra, owners, source_slots):
+def per_device_gathered(spectra, owners, source_slots):
     length = spectra.shape[3]
     width = spectra.shape[2]
     band_table = band_matrix(length, HALF)
@@ -83,7 +89,280 @@
     )
 
 
+def constant_tables(length):
+    low = np.arange(length // 2)
+    mirror = np.where(low == 0, length // 2, length - low)
+    order = np.stack([low.reshape(-1, PAIRS), mirror.reshape(-1, PAIRS)], axis=1).reshape(-1)
+    places = np.arange(length)
+    regroup = (order[:, None] == places[None, :]).astype(np.float32)
+    near = (np.abs(places[:, None] - places[None, :]) <= HALF).astype(np.float32)
+    share = 1.0 / near.sum(axis=0, keepdims=True)
+    angle = (low[:, None] * places[None, :] % length) * (2.0 * math.pi / length)
+    cosine = np.cos(angle) / length
+    sine = -np.sin(angle) / length
+    sine[0] = np.where(places % 2 == 0, 1.0, -1.0) / length
+    table = np.concatenate([cosine, sine], axis=0).astype(np.float32)
+    high = table.astype(jnp.bfloat16)
+    rest = (table - high.astype(np.float32)).astype(jnp.bfloat16)
+    return (
+        regroup.astype(jnp.bfloat16),
+        near.astype(jnp.bfloat16),
+        share.astype(np.float32),
+        high,
+        rest,
+    )
+
+
+def split(value):
+    high = value.astype(jnp.bfloat16)
+    return high, (value - high.astype(jnp.float32)).astype(jnp.bfloat16)
+
+
+def dot(a, b):
+    return jnp.dot(a, b, preferred_element_type=jnp.float32)
+
+
+def kernel(
+    n_recv, n_tm, windows, width, length,
+    x_ref, owners_ref, slots_ref, regroup_ref, near_ref, share_ref, high_ref, rest_ref,
+    out_ref,
+    outgoing, arrived, plain, sources, cross, folded, landed,
+    send_sem, recv_sem, send2_sem, recv2_sem,
+):
+    f32, bf16 = jnp.float32, jnp.bfloat16
+    devices = n_recv * n_tm
+    rows = windows * width
+    lanes = n_recv * BINS
+    my_recv, my_tm = lax.axis_index("recv"), lax.axis_index("tm")
+    me = my_recv * n_tm + my_tm
+
+    def partner(step, sign):
+        other_recv = lax.rem(my_recv + sign * lax.rem(step, n_recv) + n_recv, n_recv)
+        other_tm = lax.rem(my_tm + sign * (step // n_recv) + n_tm, n_tm)
+        return other_recv, other_tm
+
+    barrier = pltpu.get_barrier_semaphore()
+
+    def greet(step, carry):
+        other_recv, other_tm = partner(step, 1)
+        pl.semaphore_signal(
+            barrier, inc=1, device_id={"recv": other_recv, "tm": other_tm}, device_id_type=MESH
+        )
+        return carry
+
+    lax.fori_loop(1, devices, greet, 0)
+
+    real = x_ref[0].astype(f32).reshape(rows, length)
+    imag = x_ref[1].astype(f32).reshape(rows, length)
+    energy_high, energy_rest = split(real * real + imag * imag)
+    near = near_ref[...]
+    smooth = (dot(energy_high, near) + dot(energy_rest, near)) * share_ref[...]
+    gain = lax.rsqrt(smooth + epsilon)
+    regroup = regroup_ref[...]
+    for part, value in enumerate((real, imag)):
+        white = (value * gain).astype(bf16)
+        outgoing[:, part * rows : (part + 1) * rows] = lax.dot_general(
+            regroup, white, NT, preferred_element_type=f32
+        ).astype(bf16)
+
+    def bins_of(device):
+        return pl.ds(pl.multiple_of(device * BINS, BINS), BINS)
+
+    def first_copy(step):
+        other_recv, other_tm = partner(step, 1)
+        return pltpu.make_async_remote_copy(
+            src_ref=outgoing.at[bins_of(other_recv * n_tm + other_tm)],
+            dst_ref=arrived.at[my_tm, bins_of(my_recv)],
+            send_sem=send_sem.at[step],
+            recv_sem=recv_sem.at[step],
+            device_id={"recv": other_recv, "tm": other_tm},
+            device_id_type=MESH,
+        )
+
+    def first_arrival(step):
+        other_recv, other_tm = partner(step, -1)
+        return pltpu.make_async_remote_copy(
+            src_ref=outgoing.at[bins_of(other_recv * n_tm + other_tm)],
+            dst_ref=arrived.at[other_tm, bins_of(other_recv)],
+            send_sem=send_sem.at[step],
+            recv_sem=recv_sem.at[step],
+            device_id={"recv": other_recv, "tm": other_tm},
+            device_id_type=MESH,
+        )
+
+    pl.semaphore_wait(barrier, devices - 1)
+
+    def send_first(step, carry):
+        first_copy(step).start()
+        return carry
+
+    lax.fori_loop(1, devices, send_first, 0)
+    arrived[my_tm, bins_of(my_recv), :] = outgoing[bins_of(me), :]
+
+    cross[...] = jnp.zeros_like(cross)
+    place_in = lax.broadcasted_iota(jnp.int32, (lanes, lanes), 0)
+    place_out = lax.broadcasted_iota(jnp.int32, (lanes, lanes), 1)
+    same_bin = lax.rem(place_in, BINS) == lax.rem(place_out, BINS)
+
+    def stage(turn, carry):
+        def wait_first(step, inner):
+            first_arrival(step).wait_recv()
+            return inner
+
+        lax.fori_loop(jnp.maximum(turn * n_recv, 1), (turn + 1) * n_recv, wait_first, 0)
+        group_tm = lax.rem(my_tm - turn + n_tm, n_tm)
+        turned = jnp.transpose(arrived[group_tm].astype(f32))
+        plain[...] = turned
+        turned = turned.astype(bf16)
+        for block in range(STEPS):
+            owned = (place_in // BINS == owners_ref[block]) & same_bin
+            sources[block] = dot(turned, owned.astype(f32).astype(bf16))
+        for block in range(STEPS):
+
+            def window(w, sums):
+                first = pl.multiple_of(w * width, width)
+                x_real = plain[pl.ds(first, width), :]
+                x_imag = plain[pl.ds(first + rows, width), :]
+                s_real = sources[block, pl.ds(first, width), :]
+                s_imag = sources[block, pl.ds(first + rows, width), :]
+                out = []
+                for slot in range(width):
+                    a_real = s_real[slot : slot + 1, :]
+                    a_imag = s_imag[slot : slot + 1, :]
+                    out.append(sums[2 * slot] + a_real * x_real + a_imag * x_imag)
+                    out.append(sums[2 * slot + 1] + a_real * x_imag - a_imag * x_real)
+                return tuple(out)
+
+            zero = jnp.zeros((width, lanes), f32)
+            sums = lax.fori_loop(0, windows, window, (zero,) * (2 * width), unroll=2)
+            for slot in range(width):
+                for part in range(2):
+                    first = ((block * 2 + part) * width + slot) * width
+                    cross[first : first + width, :] += sums[2 * slot + part]
+        return carry
+
+    lax.fori_loop(0, n_tm, stage, 0)
+
+    by_bin = jnp.transpose(cross[...])
+    tile = 2 * width * width
+    lane = lax.broadcasted_iota(jnp.int32, (PAIRS, tile), 1)
+    row = lax.broadcasted_iota(jnp.int32, (PAIRS, tile), 0)
+    is_real = lane < width * width
+    lone = (row + me) == 0
+    for recv in range(n_recv):
+        for tm in range(n_tm):
+            column = slice(tm * tile, (tm + 1) * tile)
+            bottom = by_bin[recv * BINS : recv * BINS + PAIRS, column]
+            mirror = by_bin[recv * BINS + PAIRS : (recv + 1) * BINS, column]
+            pair = jnp.where(is_real, bottom + mirror, bottom - mirror)
+            alone = jnp.where(is_real, bottom, pltpu.roll(mirror, width * width, 1))
+            first = (recv * n_tm + tm) * PAIRS
+            folded[first : first + PAIRS, :] = jnp.where(lone, alone, pair)
+
+    def pairs_of(device):
+        return pl.ds(pl.multiple_of(device * PAIRS, PAIRS), PAIRS)
+
+    def second_copy(step, sign):
+        other_recv, other_tm = partner(step, sign)
+        other = other_recv * n_tm + other_tm
+        return pltpu.make_async_remote_copy(
+            src_ref=folded.at[pairs_of(other)],
+            dst_ref=landed.at[pairs_of(me if sign > 0 else other)],
+            send_sem=send2_sem.at[step],
+            recv_sem=recv2_sem.at[step],
+            device_id={"recv": other_recv, "tm": other_tm},
+            device_id_type=MESH,
+        )
+
+    def send_second(step, carry):
+        second_copy(step, 1).start()
+        return carry
+
+    lax.fori_loop(1, devices, send_second, 0)
+    landed[pairs_of(me), :] = folded[pairs_of(me), :]
+
+    to = lax.broadcasted_iota(jnp.int32, (tile, tile), 0)
+    frm = lax.broadcasted_iota(jnp.int32, (tile, tile), 1)
+    to_slot = lax.rem(to // width, width)
+    wanted = jnp.zeros_like(to)
+    for j in range(width):
+        wanted = jnp.where(to_slot == j, slots_ref[my_tm, j], wanted)
+    picks = (
+        (to // (width * width) == frm // (width * width))
+        & (lax.rem(to, width) == lax.rem(frm, width))
+        & (lax.rem(frm // width, width) == wanted)
+    ).astype(f32).astype(bf16)
+
+    def wait_second(step, carry):
+        second_copy(step, -1).wait_recv()
+        return carry
+
+    lax.fori_loop(1, devices, wait_second, 0)
+
+    square = width * width
+    flat_high, flat_rest = [
+        jnp.concatenate([picked[:square], picked[square:]], axis=1).astype(bf16)
+        for picked in (dot(picks, half) for half in split(jnp.transpose(landed[...])))
+    ]
+    high = high_ref[...]
+    lags = dot(flat_high, high) + (dot(flat_rest, high) + dot(flat_high, rest_ref[...]))
+    out_ref[...] = lags.reshape(width, width, length)
+
+    def wait_sent(step, carry):
+        first_copy(step).wait_send()
+        second_copy(step, 1).wait_send()
+        return carry
+
+    lax.fori_loop(1, devices, wait_sent, 0)
+
+
+def per_device_split(n_recv, n_tm, spectra, owners, source_slots):
+    _, windows, width, length = spectra.shape
+    devices = n_recv * n_tm
+    lanes = n_recv * BINS
+    tile = 2 * width * width
+    rows = windows * width
+    vmem = pl.BlockSpec(memory_space=pltpu.VMEM)
+    smem = pl.BlockSpec(memory_space=pltpu.SMEM)
+
+    def body(*refs):
+        kernel(n_recv, n_tm, windows, width, length, *refs)
+
+    return pl.pallas_call(
+        body,
+        out_shape=jax.ShapeDtypeStruct((width, width, length), jnp.float32),
+        in_specs=[vmem, smem, smem, vmem, vmem, vmem, vmem, vmem],
+        out_specs=vmem,
+        scratch_shapes=[
+            pltpu.VMEM((length, 2 * rows), jnp.bfloat16),
+            pltpu.VMEM((n_tm, lanes, 2 * rows), jnp.bfloat16),
+            pltpu.VMEM((2 * rows, lanes), jnp.float32),
+            pltpu.VMEM((STEPS, 2 * rows, lanes), jnp.float32),
+            pltpu.VMEM((STEPS * tile, lanes), jnp.float32),
+            pltpu.VMEM((devices * PAIRS, tile), jnp.float32),
+            pltpu.VMEM((devices * PAIRS, tile), jnp.float32),
+            pltpu.SemaphoreType.DMA((devices,)),
+            pltpu.SemaphoreType.DMA((devices,)),
+            pltpu.SemaphoreType.DMA((devices,)),
+            pltpu.SemaphoreType.DMA((devices,)),
+        ],
+        compiler_params=pltpu.CompilerParams(
+            collective_id=0, has_side_effects=True, vmem_limit_bytes=32 * 1024 * 1024
+        ),
+        name="whiten_exchange_correlate",
+    )(spectra, owners, source_slots, *(jnp.asarray(t) for t in constant_tables(length)))
+
+
 def solution(mesh):
+    n_recv, n_tm = mesh.shape["recv"], mesh.shape["tm"]
+
+    def per_device(spectra, owners, source_slots):
+        _, _, width, length = spectra.shape
+        slots = source_slots.shape[1]
+        if n_recv * n_tm * BINS == length and n_tm == STEPS and slots == width:
+            return per_device_split(n_recv, n_tm, spectra, owners, source_slots)
+        return per_device_gathered(spectra, owners, source_slots)
+
     in_specs = (P(None, "tm", "recv", None), P(), P())
     out_specs = P("tm", "recv", None)
     return jax.shard_map(

time: 249 us -> 40.4 us (0.16)
  waiting for transfers between devices: 125 us -> 0 us
  matrix products: 62.6 us -> 0 us
  local copies, waits for them, and re-layouts: 42.1 us -> 7.88 us
  Pallas kernels: 0 us -> 32.1 us
  between operations: 16.1 us -> 0.02 us
    psum x1 -> x0, waiting for transfers between devices: 105 us -> none  [broadcast(): return lax.psum(kept, axis)]
    dot_general x23 -> x0, matrix products: 62.6 us -> none  [the longest x4 14.8 us: per_device(): jnp.einsum('wsf,wrf->srf', arrived[1], whitened[1], preferred_element_typ...]
    pallas_call x0 -> x1, Pallas kernels: none -> 32.1 us  [per_device_split(): pl.pallas_call(body, out_shape=jax.ShapeDtypeStruct((width, width, length...]
    reduce_scatter x1 -> x0, waiting for transfers between devices: 20.9 us -> none  [per_device(): lax.psum_scatter(inverse_lags(cross_real, cross_imag, cosine, sine), 'tm'...]
    squeeze x13 -> x0, local copies, waits for them, and re-layouts: 20.3 us -> none  [the longest x6 11.4 us: per_device(): arrived[1]]
    add x4 -> x0, local copies, waits for them, and re-layouts: 10.8 us -> none  [per_device(): jnp.einsum('wsf,wrf->srf', arrived[0], whitened[0], preferred_element_typ...]
    sub x4 -> x0, local copies, waits for them, and re-layouts: 9.53 us -> none  [per_device(): jnp.einsum('wsf,wrf->srf', arrived[0], whitened[1], preferred_element_typ...]
    unnamed x22 -> x17, local copies, waits for them, and re-layouts: 0.05 us -> 7.88 us
  transfers between devices with their start and end apart: 2 -> 0, of which waited for: 2 -> 0; matrix products, arithmetic and copies ran while one was open for 1% -> 0% of each run, Pallas kernels for 0% -> 0%
where the time goes in v1:
time: 40.4 us; the launch traced here: 40 us
  Pallas kernels  32.1 us (79%)
  local copies, waits for them, and re-layouts  7.88 us (20%)
    pallas_call x1, Pallas kernels, per_device_split(): pl.pallas_call(body, out_shape=jax.ShapeDtypeStruct((width, width, length...  32.1 us
    unnamed x17, local copies, waits for them, and re-layouts  7.88 us

profile of v1, /device:TPU:0, one launch (start us, length us, event | category | flops | bytes accessed | tf_op | source)
XLA Modules:
  0.0 40.0 jit_solution(15881496448186818101)
XLA Ops:
  0.0 0.0 copy-start.6
  0.0 0.7 %copy-done.6 = f32[1,512]{1,0:T(1,128)S(1)} copy-done((f32[1,512]{1,0:T(1,128)S(1)}, f32[1,512]{1,0:T(1,128)}, u32[]{:S(2)}) %copy-start.6) | copy-done | bytes 2072
  0.7 0.0 copy-start
  0.7 1.0 %copy-done = bf16[2,32,8,512]{3,2,1,0:T(8,128)(2,1)S(1)} copy-done((bf16[2,32,8,512]{3,2,1,0:T(8,128)(2,1)S(1)}, bf16[2,32,8,512]{3,2,1,0:T(8,128)(2,1)}, u32[]{:S(2)}) %copy-start) | copy-done | bytes 524312
  1.7 0.0 copy-start.1
  1.7 1.0 %copy-done.1 = bf16[512,512]{1,0:T(8,128)(2,1)S(1)} copy-done((bf16[512,512]{1,0:T(8,128)(2,1)S(1)}, bf16[512,512]{1,0:T(8,128)(2,1)}, u32[]{:S(2)}) %copy-start.1) | copy-done | bytes 524312
  2.8 0.0 copy-start.2
  2.8 1.0 %copy-done.2 = bf16[512,512]{1,0:T(8,128)(2,1)S(1)} copy-done((bf16[512,512]{1,0:T(8,128)(2,1)S(1)}, bf16[512,512]{1,0:T(8,128)(2,1)}, u32[]{:S(2)}) %copy-start.2) | copy-done | bytes 524312
  3.8 0.0 copy-start.3
  3.8 1.0 %copy-done.3 = bf16[512,512]{1,0:T(8,128)(2,1)S(1)} copy-done((bf16[512,512]{1,0:T(8,128)(2,1)S(1)}, bf16[512,512]{1,0:T(8,128)(2,1)}, u32[]{:S(2)}) %copy-start.3) | copy-done | bytes 524312
  4.9 0.0 copy-start.4
  4.9 1.0 %copy-done.4 = bf16[512,512]{1,0:T(8,128)(2,1)S(1)} copy-done((bf16[512,512]{1,0:T(8,128)(2,1)S(1)}, bf16[512,512]{1,0:T(8,128)(2,1)}, u32[]{:S(2)}) %copy-start.4) | copy-done | bytes 524312
  5.9 0.0 copy-start.5
  5.9 0.7 %copy-done.5 = s32[4,8]{1,0:T(4,128)S(1)} copy-done((s32[4,8]{1,0:T(4,128)S(1)}, s32[4,8]{1,0:T(4,128)}, u32[]{:S(2)}) %copy-start.5) | copy-done | bytes 152
  6.6 0.0 copy-start.7
  6.6 0.7 %copy-done.7 = s32[4]{0:T(128)S(1)} copy-done((s32[4]{0:T(128)S(1)}, s32[4]{0:T(128)}, u32[]{:S(2)}) %copy-start.7) | copy-done | bytes 40
  7.2 32.1 %whiten_exchange_correlate.1 = f32[8,8,512]{2,1,0:T(8,128)S(1)} custom-call(bf16[2,32,8,512]{3,2,1,0:T(8,128)(2,1)S(1)} %copy-done, s32[4]{0:T(128)S(1)} %copy-done.7, s32[4,8]{1,0:T(4,128)S(1)} %copy-done.5, bf16[512,512]{1,0:T(8,128)(2,1)S(1)} %copy-done.4, bf16[512,512]{1,0:T(8,128)(2,1)S(1)} %copy-done.3, f32[1,512]{1,0:T(1,128)S(1)} %copy-done.6, ...), custom_call_target="tpu_custom_call" | custom-call | tf_op jit(solution)/shard_map/whiten_exchange_correlate/pallas_call | solution.py:331
  39.3 0.7 %copy.10 = f32[8,8,512]{2,1,0:T(8,128)} copy(f32[8,8,512]{2,1,0:T(8,128)S(1)} %whiten_exchange_correlate.1) | data formatting | bytes 262144
Async XLA Ops:
  0.0 0.7 %copy-start.6 = (f32[1,512]{1,0:T(1,128)S(1)}, f32[1,512]{1,0:T(1,128)}, u32[]{:S(2)}) copy-start(f32[1,512]{1,0:T(1,128)} %constant.12.clone.refs_5_) | copy-start | bytes 6148
  0.7 1.0 %copy-start = (bf16[2,32,8,512]{3,2,1,0:T(8,128)(2,1)S(1)}, bf16[2,32,8,512]{3,2,1,0:T(8,128)(2,1)}, u32[]{:S(2)}) copy-start(bf16[2,32,8,512]{3,2,1,0:T(8,128)(2,1)} %refs_0_.1) | copy-start | bytes 1572868
  1.7 1.0 %copy-start.1 = (bf16[512,512]{1,0:T(8,128)(2,1)S(1)}, bf16[512,512]{1,0:T(8,128)(2,1)}, u32[]{:S(2)}) copy-start(bf16[512,512]{1,0:T(8,128)(2,1)} %constant.14.clone.refs_7_) | copy-start | bytes 1572868
  2.8 1.0 %copy-start.2 = (bf16[512,512]{1,0:T(8,128)(2,1)S(1)}, bf16[512,512]{1,0:T(8,128)(2,1)}, u32[]{:S(2)}) copy-start(bf16[512,512]{1,0:T(8,128)(2,1)} %constant.13.clone.refs_6_) | copy-start | bytes 1572868
  3.8 1.0 %copy-start.3 = (bf16[512,512]{1,0:T(8,128)(2,1)S(1)}, bf16[512,512]{1,0:T(8,128)(2,1)}, u32[]{:S(2)}) copy-start(bf16[512,512]{1,0:T(8,128)(2,1)} %constant.11.clone.refs_4_) | copy-start | bytes 1572868
  4.9 1.0 %copy-start.4 = (bf16[512,512]{1,0:T(8,128)(2,1)S(1)}, bf16[512,512]{1,0:T(8,128)(2,1)}, u32[]{:S(2)}) copy-start(bf16[512,512]{1,0:T(8,128)(2,1)} %constant.10.clone.refs_3_) | copy-start | bytes 1572868
  5.9 0.7 %copy-start.5 = (s32[4,8]{1,0:T(4,128)S(1)}, s32[4,8]{1,0:T(4,128)}, u32[]{:S(2)}) copy-start(s32[4,8]{1,0:T(4,128)} %refs_2_.1) | copy-start | bytes 388
  6.6 0.7 %copy-start.7 = (s32[4]{0:T(128)S(1)}, s32[4]{0:T(128)}, u32[]{:S(2)}) copy-start(s32[4]{0:T(128)} %refs_1_.1) | copy-start | bytes 52

commit v2 on v1

--- a/solution.py
+++ b/solution.py
@@ -89,28 +89,14 @@
     )
 
 
-def constant_tables(length):
+def folded_table(length):
     low = np.arange(length // 2)
-    mirror = np.where(low == 0, length // 2, length - low)
-    order = np.stack([low.reshape(-1, PAIRS), mirror.reshape(-1, PAIRS)], axis=1).reshape(-1)
     places = np.arange(length)
-    regroup = (order[:, None] == places[None, :]).astype(np.float32)
-    near = (np.abs(places[:, None] - places[None, :]) <= HALF).astype(np.float32)
-    share = 1.0 / near.sum(axis=0, keepdims=True)
     angle = (low[:, None] * places[None, :] % length) * (2.0 * math.pi / length)
     cosine = np.cos(angle) / length
     sine = -np.sin(angle) / length
     sine[0] = np.where(places % 2 == 0, 1.0, -1.0) / length
-    table = np.concatenate([cosine, sine], axis=0).astype(np.float32)
-    high = table.astype(jnp.bfloat16)
-    rest = (table - high.astype(np.float32)).astype(jnp.bfloat16)
-    return (
-        regroup.astype(jnp.bfloat16),
-        near.astype(jnp.bfloat16),
-        share.astype(np.float32),
-        high,
-        rest,
-    )
+    return np.concatenate([cosine, sine], axis=0).astype(np.float32)
 
 
 def split(value):
@@ -118,14 +104,20 @@
     return high, (value - high.astype(jnp.float32)).astype(jnp.bfloat16)
 
 
+def as_ones(mask):
+    return mask.astype(jnp.float32).astype(jnp.bfloat16)
+
+
 def dot(a, b):
     return jnp.dot(a, b, preferred_element_type=jnp.float32)
 
 
 def kernel(
     n_recv, n_tm, windows, width, length,
-    x_ref, owners_ref, slots_ref, regroup_ref, near_ref, share_ref, high_ref, rest_ref,
+    x_hbm, owners_hbm, slots_hbm, table_hbm,
     out_ref,
+    x_ref, owners_ref, slots_ref, table_ref, load_sem,
+    regroup_ref,
     outgoing, arrived, plain, sources, cross, folded, landed,
     send_sem, recv_sem, send2_sem, recv2_sem,
 ):
@@ -134,7 +126,17 @@
     rows = windows * width
     lanes = n_recv * BINS
     my_recv, my_tm = lax.axis_index("recv"), lax.axis_index("tm")
-    me = my_recv * n_tm + my_tm
+    me = my_tm * n_recv + my_recv
+
+    places = (
+        (x_hbm, x_ref), (owners_hbm, owners_ref), (slots_hbm, slots_ref), (table_hbm, table_ref),
+    )
+    loads = [
+        pltpu.make_async_copy(source, target, load_sem.at[number])
+        for number, (source, target) in enumerate(places)
+    ]
+    for load in loads:
+        load.start()
 
     def partner(step, sign):
         other_recv = lax.rem(my_recv + sign * lax.rem(step, n_recv) + n_recv, n_recv)
@@ -152,18 +154,22 @@
 
     lax.fori_loop(1, devices, greet, 0)
 
+    position = lax.broadcasted_iota(jnp.int32, (1, length), 1)
+    count = jnp.minimum(position, HALF) + jnp.minimum(length - 1 - position, HALF) + 1
+    share = 1.0 / count.astype(f32)
+    row = lax.broadcasted_iota(jnp.int32, (length, length), 0)
+    column = lax.broadcasted_iota(jnp.int32, (length, length), 1)
+    near = as_ones(jnp.abs(row - column) <= HALF)
+    low = row // BINS * PAIRS + lax.rem(row, PAIRS)
+    mirror = jnp.where(low == 0, length // 2, length - low)
+    regroup_ref[...] = as_ones(jnp.where(lax.rem(row, BINS) < PAIRS, low, mirror) == column)
+    loads[0].wait()
     real = x_ref[0].astype(f32).reshape(rows, length)
     imag = x_ref[1].astype(f32).reshape(rows, length)
     energy_high, energy_rest = split(real * real + imag * imag)
-    near = near_ref[...]
-    smooth = (dot(energy_high, near) + dot(energy_rest, near)) * share_ref[...]
+    smooth = (dot(energy_high, near) + dot(energy_rest, near)) * share
     gain = lax.rsqrt(smooth + epsilon)
-    regroup = regroup_ref[...]
-    for part, value in enumerate((real, imag)):
-        white = (value * gain).astype(bf16)
-        outgoing[:, part * rows : (part + 1) * rows] = lax.dot_general(
-            regroup, white, NT, preferred_element_type=f32
-        ).astype(bf16)
+    white = jnp.concatenate([real * gain, imag * gain], axis=0).astype(bf16)
 
     def bins_of(device):
         return pl.ds(pl.multiple_of(device * BINS, BINS), BINS)
@@ -171,7 +177,7 @@
     def first_copy(step):
         other_recv, other_tm = partner(step, 1)
         return pltpu.make_async_remote_copy(
-            src_ref=outgoing.at[bins_of(other_recv * n_tm + other_tm)],
+            src_ref=outgoing.at[bins_of(other_tm * n_recv + other_recv)],
             dst_ref=arrived.at[my_tm, bins_of(my_recv)],
             send_sem=send_sem.at[step],
             recv_sem=recv_sem.at[step],
@@ -182,7 +188,7 @@
     def first_arrival(step):
         other_recv, other_tm = partner(step, -1)
         return pltpu.make_async_remote_copy(
-            src_ref=outgoing.at[bins_of(other_recv * n_tm + other_tm)],
+            src_ref=outgoing.at[bins_of(other_tm * n_recv + other_recv)],
             dst_ref=arrived.at[other_tm, bins_of(other_recv)],
             send_sem=send_sem.at[step],
             recv_sem=recv_sem.at[step],
@@ -196,10 +202,17 @@
         first_copy(step).start()
         return carry
 
-    lax.fori_loop(1, devices, send_first, 0)
+    for turn in range(n_tm):
+        group = pl.ds(pl.multiple_of(lax.rem(my_tm + turn, n_tm) * lanes, lanes), lanes)
+        outgoing[group, :] = lax.dot_general(
+            regroup_ref[group, :], white, NT, preferred_element_type=f32
+        ).astype(bf16)
+        lax.fori_loop(max(turn * n_recv, 1), (turn + 1) * n_recv, send_first, 0)
     arrived[my_tm, bins_of(my_recv), :] = outgoing[bins_of(me), :]
 
     cross[...] = jnp.zeros_like(cross)
+    for load in loads[1:]:
+        load.wait()
     place_in = lax.broadcasted_iota(jnp.int32, (lanes, lanes), 0)
     place_out = lax.broadcasted_iota(jnp.int32, (lanes, lanes), 1)
     same_bin = lax.rem(place_in, BINS) == lax.rem(place_out, BINS)
@@ -216,7 +229,7 @@
         turned = turned.astype(bf16)
         for block in range(STEPS):
             owned = (place_in // BINS == owners_ref[block]) & same_bin
-            sources[block] = dot(turned, owned.astype(f32).astype(bf16))
+            sources[block] = dot(turned, as_ones(owned))
         for block in range(STEPS):
 
             def window(w, sums):
@@ -256,7 +269,7 @@
             mirror = by_bin[recv * BINS + PAIRS : (recv + 1) * BINS, column]
             pair = jnp.where(is_real, bottom + mirror, bottom - mirror)
             alone = jnp.where(is_real, bottom, pltpu.roll(mirror, width * width, 1))
-            first = (recv * n_tm + tm) * PAIRS
+            first = (tm * n_recv + recv) * PAIRS
             folded[first : first + PAIRS, :] = jnp.where(lone, alone, pair)
 
     def pairs_of(device):
@@ -264,7 +277,7 @@
 
     def second_copy(step, sign):
         other_recv, other_tm = partner(step, sign)
-        other = other_recv * n_tm + other_tm
+        other = other_tm * n_recv + other_recv
         return pltpu.make_async_remote_copy(
             src_ref=folded.at[pairs_of(other)],
             dst_ref=landed.at[pairs_of(me if sign > 0 else other)],
@@ -287,11 +300,12 @@
     wanted = jnp.zeros_like(to)
     for j in range(width):
         wanted = jnp.where(to_slot == j, slots_ref[my_tm, j], wanted)
-    picks = (
+    picks = as_ones(
         (to // (width * width) == frm // (width * width))
         & (lax.rem(to, width) == lax.rem(frm, width))
         & (lax.rem(frm // width, width) == wanted)
-    ).astype(f32).astype(bf16)
+    )
+    high, rest = split(table_ref[...])
 
     def wait_second(step, carry):
         second_copy(step, -1).wait_recv()
@@ -304,8 +318,7 @@
         jnp.concatenate([picked[:square], picked[square:]], axis=1).astype(bf16)
         for picked in (dot(picks, half) for half in split(jnp.transpose(landed[...])))
     ]
-    high = high_ref[...]
-    lags = dot(flat_high, high) + (dot(flat_rest, high) + dot(flat_high, rest_ref[...]))
+    lags = dot(flat_high, high) + (dot(flat_rest, high) + dot(flat_high, rest))
     out_ref[...] = lags.reshape(width, width, length)
 
     def wait_sent(step, carry):
@@ -323,7 +336,12 @@
     tile = 2 * width * width
     rows = windows * width
     vmem = pl.BlockSpec(memory_space=pltpu.VMEM)
-    smem = pl.BlockSpec(memory_space=pltpu.SMEM)
+    operands = (spectra, owners, source_slots, jnp.asarray(folded_table(length)))
+    scalars = (owners, source_slots)
+    held = [
+        (pltpu.SMEM if any(one is s for s in scalars) else pltpu.VMEM)(one.shape, one.dtype)
+        for one in operands
+    ]
 
     def body(*refs):
         kernel(n_recv, n_tm, windows, width, length, *refs)
@@ -331,9 +349,12 @@
     return pl.pallas_call(
         body,
         out_shape=jax.ShapeDtypeStruct((width, width, length), jnp.float32),
-        in_specs=[vmem, smem, smem, vmem, vmem, vmem, vmem, vmem],
+        in_specs=[pl.BlockSpec(memory_space=pltpu.MemorySpace.HBM)] * len(operands),
         out_specs=vmem,
         scratch_shapes=[
+            *held,
+            pltpu.SemaphoreType.DMA((len(operands),)),
+            pltpu.VMEM((length, length), jnp.bfloat16),
             pltpu.VMEM((length, 2 * rows), jnp.bfloat16),
             pltpu.VMEM((n_tm, lanes, 2 * rows), jnp.bfloat16),
             pltpu.VMEM((2 * rows, lanes), jnp.float32),
@@ -346,11 +367,9 @@
             pltpu.SemaphoreType.DMA((devices,)),
             pltpu.SemaphoreType.DMA((devices,)),
         ],
-        compiler_params=pltpu.CompilerParams(
-            collective_id=0, has_side_effects=True, vmem_limit_bytes=32 * 1024 * 1024
-        ),
+        compiler_params=pltpu.CompilerParams(collective_id=0, has_side_effects=True),
         name="whiten_exchange_correlate",
-    )(spectra, owners, source_slots, *(jnp.asarray(t) for t in constant_tables(length)))
+    )(*operands)
 
 
 def solution(mesh):

time: 40.4 us -> 34.2 us (0.85)
  local copies, waits for them, and re-layouts: 7.88 us -> 1.57 us
    unnamed x17 -> x1, local copies, waits for them, and re-layouts: 7.88 us -> 1.57 us
where the time goes in v2:
time: 34.2 us; the launch traced here: 34 us
  Pallas kernels  32.4 us (95%)
  local copies, waits for them, and re-layouts  1.57 us (5%)
    pallas_call x1, Pallas kernels, per_device_split(): pl.pallas_call(body, out_shape=jax.ShapeDtypeStruct((width, width, length...  32.4 us
    unnamed x1, local copies, waits for them, and re-layouts  1.57 us

profile of v2, /device:TPU:0, one launch (start us, length us, event | category | flops | bytes accessed | tf_op | source)
XLA Modules:
  0.0 34.0 jit_solution(9470161705691204140)
XLA Ops:
  0.0 32.4 %whiten_exchange_correlate.1 = f32[8,8,512]{2,1,0:T(8,128)} custom-call(bf16[2,32,8,512]{3,2,1,0:T(8,128)(2,1)} %refs_0_.1, s32[4]{0:T(128)} %refs_1_.1, s32[4,8]{1,0:T(4,128)} %refs_2_.1, f32[512,512]{1,0:T(8,128)} %constant.2.clone.refs_3_), custom_call_target="tpu_custom_call" | custom-call | tf_op jit(solution)/shard_map/whiten_exchange_correlate/pallas_call | solution.py:349
  32.4 1.6 %copy.6 = f32[8,8,512]{2,1,0:T(8,128)} copy(f32[8,8,512]{2,1,0:T(8,128)} %whiten_exchange_correlate.1) | data formatting | bytes 262144

commit v3 on v2

--- a/solution.py
+++ b/solution.py
@@ -9,6 +9,7 @@
 from jax.sharding import PartitionSpec as P
 
 HALF = 64
+LANES = 128
 STEPS = 4
 BINS = 16
 PAIRS = BINS // 2
@@ -117,13 +118,13 @@
     x_hbm, owners_hbm, slots_hbm, table_hbm,
     out_ref,
     x_ref, owners_ref, slots_ref, table_ref, load_sem,
-    regroup_ref,
-    outgoing, arrived, plain, sources, cross, folded, landed,
+    regroup_ref, white_ref, outgoing, arrived, picked, source, receiver, cross, folded, landed,
     send_sem, recv_sem, send2_sem, recv2_sem,
 ):
     f32, bf16 = jnp.float32, jnp.bfloat16
     devices = n_recv * n_tm
     rows = windows * width
+    terms = 2 * windows
     lanes = n_recv * BINS
     my_recv, my_tm = lax.axis_index("recv"), lax.axis_index("tm")
     me = my_tm * n_recv + my_recv
@@ -169,7 +170,21 @@
     energy_high, energy_rest = split(real * real + imag * imag)
     smooth = (dot(energy_high, near) + dot(energy_rest, near)) * share
     gain = lax.rsqrt(smooth + epsilon)
-    white = jnp.concatenate([real * gain, imag * gain], axis=0).astype(bf16)
+    for part, value in enumerate((real, imag)):
+        scaled = value * gain
+        for tile in range(length // LANES):
+            white_ref[tile, part * rows : (part + 1) * rows, :] = scaled[
+                :, tile * LANES : (tile + 1) * LANES
+            ]
+    white = jnp.concatenate(
+        [
+            jnp.concatenate(
+                [white_ref[tile, pl.ds(c, terms, stride=width), :] for c in range(width)], axis=0
+            ).astype(bf16)
+            for tile in range(length // LANES)
+        ],
+        axis=1,
+    )
 
     def bins_of(device):
         return pl.ds(pl.multiple_of(device * BINS, BINS), BINS)
@@ -210,67 +225,55 @@
         lax.fori_loop(max(turn * n_recv, 1), (turn + 1) * n_recv, send_first, 0)
     arrived[my_tm, bins_of(my_recv), :] = outgoing[bins_of(me), :]
 
-    cross[...] = jnp.zeros_like(cross)
     for load in loads[1:]:
         load.wait()
-    place_in = lax.broadcasted_iota(jnp.int32, (lanes, lanes), 0)
-    place_out = lax.broadcasted_iota(jnp.int32, (lanes, lanes), 1)
-    same_bin = lax.rem(place_in, BINS) == lax.rem(place_out, BINS)
-
-    def stage(turn, carry):
-        def wait_first(step, inner):
-            first_arrival(step).wait_recv()
-            return inner
-
-        lax.fori_loop(jnp.maximum(turn * n_recv, 1), (turn + 1) * n_recv, wait_first, 0)
-        group_tm = lax.rem(my_tm - turn + n_tm, n_tm)
-        turned = jnp.transpose(arrived[group_tm].astype(f32))
-        plain[...] = turned
-        turned = turned.astype(bf16)
-        for block in range(STEPS):
-            owned = (place_in // BINS == owners_ref[block]) & same_bin
-            sources[block] = dot(turned, as_ones(owned))
-        for block in range(STEPS):
-
-            def window(w, sums):
-                first = pl.multiple_of(w * width, width)
-                x_real = plain[pl.ds(first, width), :]
-                x_imag = plain[pl.ds(first + rows, width), :]
-                s_real = sources[block, pl.ds(first, width), :]
-                s_imag = sources[block, pl.ds(first + rows, width), :]
-                out = []
-                for slot in range(width):
-                    a_real = s_real[slot : slot + 1, :]
-                    a_imag = s_imag[slot : slot + 1, :]
-                    out.append(sums[2 * slot] + a_real * x_real + a_imag * x_imag)
-                    out.append(sums[2 * slot + 1] + a_real * x_imag - a_imag * x_real)
-                return tuple(out)
-
-            zero = jnp.zeros((width, lanes), f32)
-            sums = lax.fori_loop(0, windows, window, (zero,) * (2 * width), unroll=2)
-            for slot in range(width):
-                for part in range(2):
-                    first = ((block * 2 + part) * width + slot) * width
-                    cross[first : first + width, :] += sums[2 * slot + part]
-        return carry
-
-    lax.fori_loop(0, n_tm, stage, 0)
-
-    by_bin = jnp.transpose(cross[...])
+
+    place = lax.broadcasted_iota(jnp.int32, (STEPS * BINS, lanes), 0)
+    origin = lax.broadcasted_iota(jnp.int32, (STEPS * BINS, lanes), 1)
+    owner = jnp.zeros_like(place)
+    for block in range(STEPS):
+        owner = jnp.where(place // BINS == block, owners_ref[block], owner)
+    owned = as_ones((origin // BINS == owner) & (lax.rem(origin, BINS) == lax.rem(place, BINS)))
+
+    def wait_first(step, carry):
+        first_arrival(step).wait_recv()
+        return carry
+
+    for turn in range(n_tm):
+        lax.fori_loop(max(turn * n_recv, 1), (turn + 1) * n_recv, wait_first, 0)
+        block_in = arrived[lax.rem(my_tm - turn + n_tm, n_tm)]
+        turned = jnp.transpose(block_in.astype(f32)).astype(bf16)
+        for c in range(width):
+            receiver[turn * terms : (turn + 1) * terms, c * lanes : (c + 1) * lanes] = turned[
+                c * terms : (c + 1) * terms
+            ]
+        picked[turn] = dot(owned, block_in)
+        if (turn + 1) * terms % LANES == 0:
+            group = LANES // terms
+            tile = turn // group
+            for c in range(width):
+                source[tile, pl.ds(c, STEPS * BINS, stride=width), :] = jnp.concatenate(
+                    [
+                        picked[tile * group + member, :, c * terms : (c + 1) * terms]
+                        for member in range(group)
+                    ],
+                    axis=1,
+                )
+
+    depth = n_tm * terms
+    term_in = lax.broadcasted_iota(jnp.int32, (depth, depth), 0)
+    term_out = lax.broadcasted_iota(jnp.int32, (depth, depth), 1)
+    is_first = lax.rem(term_out, terms) < windows
+    swap = as_ones((term_in == term_out - windows) & ~is_first) - as_ones(
+        (term_in == term_out + windows) & is_first
+    )
+
     tile = 2 * width * width
     lane = lax.broadcasted_iota(jnp.int32, (PAIRS, tile), 1)
     row = lax.broadcasted_iota(jnp.int32, (PAIRS, tile), 0)
     is_real = lane < width * width
     lone = (row + me) == 0
-    for recv in range(n_recv):
-        for tm in range(n_tm):
-            column = slice(tm * tile, (tm + 1) * tile)
-            bottom = by_bin[recv * BINS : recv * BINS + PAIRS, column]
-            mirror = by_bin[recv * BINS + PAIRS : (recv + 1) * BINS, column]
-            pair = jnp.where(is_real, bottom + mirror, bottom - mirror)
-            alone = jnp.where(is_real, bottom, pltpu.roll(mirror, width * width, 1))
-            first = (tm * n_recv + recv) * PAIRS
-            folded[first : first + PAIRS, :] = jnp.where(lone, alone, pair)
+    bin_of = lax.rem(lax.broadcasted_iota(jnp.int32, (width, width * lanes), 1), BINS)
 
     def pairs_of(device):
         return pl.ds(pl.multiple_of(device * PAIRS, PAIRS), PAIRS)
@@ -291,7 +294,33 @@
         second_copy(step, 1).start()
         return carry
 
-    lax.fori_loop(1, devices, send_second, 0)
+    arrivals = receiver[...]
+    block_rows = BINS * width
+    for turn in range(n_tm):
+        block = lax.rem(my_tm + turn, n_tm)
+        chosen = pl.ds(pl.multiple_of(block * block_rows, block_rows), block_rows)
+        direct = jnp.concatenate(
+            [source[number, chosen, :] for number in range(depth // LANES)], axis=1
+        ).astype(bf16)
+        swapped = dot(direct, swap).astype(bf16)
+        for part, left in enumerate((direct, swapped)):
+            products = dot(left, arrivals)
+            sums = products[:width]
+            for number in range(1, BINS):
+                sums = jnp.where(
+                    bin_of == number, products[number * width : (number + 1) * width], sums
+                )
+            for c in range(width):
+                first = (part * width + c) * width
+                cross[first : first + width, :] = sums[:, c * lanes : (c + 1) * lanes]
+        by_bin = jnp.transpose(cross[...])
+        for recv in range(n_recv):
+            bottom = by_bin[recv * BINS : recv * BINS + PAIRS]
+            mirror = by_bin[recv * BINS + PAIRS : (recv + 1) * BINS]
+            pair = jnp.where(is_real, bottom + mirror, bottom - mirror)
+            alone = jnp.where(is_real, bottom, pltpu.roll(mirror, width * width, 1))
+            folded[pairs_of(block * n_recv + recv), :] = jnp.where(lone, alone, pair)
+        lax.fori_loop(max(turn * n_recv, 1), (turn + 1) * n_recv, send_second, 0)
     landed[pairs_of(me), :] = folded[pairs_of(me), :]
 
     to = lax.broadcasted_iota(jnp.int32, (tile, tile), 0)
@@ -302,8 +331,8 @@
         wanted = jnp.where(to_slot == j, slots_ref[my_tm, j], wanted)
     picks = as_ones(
         (to // (width * width) == frm // (width * width))
-        & (lax.rem(to, width) == lax.rem(frm, width))
-        & (lax.rem(frm // width, width) == wanted)
+        & (lax.rem(to, width) == lax.rem(frm // width, width))
+        & (lax.rem(frm, width) == wanted)
     )
     high, rest = split(table_ref[...])
 
@@ -355,11 +384,13 @@
             *held,
             pltpu.SemaphoreType.DMA((len(operands),)),
             pltpu.VMEM((length, length), jnp.bfloat16),
+            pltpu.VMEM((length // LANES, 2 * rows, LANES), jnp.float32),
             pltpu.VMEM((length, 2 * rows), jnp.bfloat16),
             pltpu.VMEM((n_tm, lanes, 2 * rows), jnp.bfloat16),
-            pltpu.VMEM((2 * rows, lanes), jnp.float32),
-            pltpu.VMEM((STEPS, 2 * rows, lanes), jnp.float32),
-            pltpu.VMEM((STEPS * tile, lanes), jnp.float32),
+            pltpu.VMEM((n_tm, STEPS * BINS, 2 * rows), jnp.float32),
+            pltpu.VMEM((n_tm * 2 * windows // LANES, STEPS * BINS * width, LANES), jnp.float32),
+            pltpu.VMEM((n_tm * 2 * windows, width * lanes), jnp.bfloat16),
+            pltpu.VMEM((tile, lanes), jnp.float32),
             pltpu.VMEM((devices * PAIRS, tile), jnp.float32),
             pltpu.VMEM((devices * PAIRS, tile), jnp.float32),
             pltpu.SemaphoreType.DMA((devices,)),

time: 34.2 us -> 31.8 us (0.930)
  Pallas kernels: 32.4 us -> 30.1 us
    pallas_call x1, Pallas kernels: 32.4 us -> 30.1 us  [per_device_split(): pl.pallas_call(body, out_shape=jax.ShapeDtypeStruct((width, width, length...]
where the time goes in v3:
time: 31.8 us; the launch traced here: 31.6 us
  Pallas kernels  30.1 us (95%)
  local copies, waits for them, and re-layouts  1.57 us (5%)
    pallas_call x1, Pallas kernels, per_device_split(): pl.pallas_call(body, out_shape=jax.ShapeDtypeStruct((width, width, length...  30.1 us
    unnamed x1, local copies, waits for them, and re-layouts  1.57 us

profile of v3, /device:TPU:0, one launch (start us, length us, event | category | flops | bytes accessed | tf_op | source)
XLA Modules:
  0.0 31.6 jit_solution(15194022597452785082)
XLA Ops:
  0.0 30.1 %whiten_exchange_correlate.1 = f32[8,8,512]{2,1,0:T(8,128)} custom-call(bf16[2,32,8,512]{3,2,1,0:T(8,128)(2,1)} %refs_0_.1, s32[4]{0:T(128)} %refs_1_.1, s32[4,8]{1,0:T(4,128)} %refs_2_.1, f32[512,512]{1,0:T(8,128)} %constant.2.clone.refs_3_), custom_call_target="tpu_custom_call" | custom-call | tf_op jit(solution)/shard_map/whiten_exchange_correlate/pallas_call | solution.py:378
  30.1 1.6 %copy.6 = f32[8,8,512]{2,1,0:T(8,128)} copy(f32[8,8,512]{2,1,0:T(8,128)} %whiten_exchange_correlate.1) | data formatting | bytes 262144
